TPU v7x, 32 devices: a whole 2x2x4 slice. The times are simulated.
32 devices in a mesh: groups: 2 (over x), rows: 4 (over y, core), cols: 4 (over z).
Axes of the slice: x: 2, y: 2, z: 4, core: 2. Of those that a mesh axis runs over, the one named last changes fastest.
Arguments:
- pair: bfloat16 [128, 64, 128], P(('groups', 'rows'), 'cols'), parts along dimension 0, may hold values from -6 to 6
- cotangent: bfloat16 [128, 64, 128], P(('groups', 'rows'), 'cols'), parts along dimension 0, may hold values from -6 to 6
- crop_length: int32 [2], P('groups'), parts along dimension 0, may hold values from 32 to 64
- gain_in: float32 [128], replicated, may hold values from 0.1 to 1.9
- w_in: bfloat16 [128, 512], replicated, may hold values from -0.5 to 0.5
- w_gate: bfloat16 [128, 128], replicated, may hold values from -0.5 to 0.5
- product_norm_gain: float32 [128], replicated, may hold values from 0.1 to 1.9
- w_out: bfloat16 [128, 128], replicated, may hold values from -0.5 to 0.5
Outputs:
- update: bfloat16 [128, 64, 128], P(('groups', 'rows'), 'cols'), parts along dimension 0
- pair_grad: bfloat16 [128, 64, 128], P(('groups', 'rows'), 'cols'), parts along dimension 0
- grad_in: float32 [256, 512], P('groups'), parts along dimension 0
- grad_gate: float32 [256, 128], P('groups'), parts along dimension 0
- grad_out: float32 [256, 128], P('groups'), parts along dimension 0
There are 2 independent parts, one for each index of `groups`. A program takes and returns all parts, laid end to end along the dimension named above; an argument that names none is the same for every part. Nothing has to cross between parts.
Inputs may be any that keep to these rules, and one draw needn't show every extreme that they name: The tokens from crop_length[0] on are padding.
All inputs are finite; a program needn't handle non-finite values.
Results may differ from a plain program's by a relative error of at most 0.02.
Values may be sent and summed in bfloat16 or wider, within the bound.
A program may use at most 128 MiB of HBM per device.

v0:
```python
import jax
import jax.numpy as jnp
from jax import lax
from jax.sharding import PartitionSpec as P


def apply_layer_norm(values, gain):
    centre = values - jnp.mean(values, axis=-1, keepdims=True)
    inverse = lax.rsqrt(jnp.mean(centre * centre, axis=-1, keepdims=True) + 1e-05)
    normed = centre * inverse
    return (normed * gain, normed, inverse)


def layer_norm_backward(upstream, gain, normed, inverse):
    scaled = upstream * gain
    return inverse * (
        scaled
        - jnp.mean(scaled, axis=-1, keepdims=True)
        - normed * jnp.mean(scaled * normed, axis=-1, keepdims=True)
    )


def per_device(pair, cotangent, crop_length, gain_in, w_in, w_gate, product_norm_gain, w_out):
    f32 = jnp.float32
    to_brain_float = jnp.bfloat16
    row_count = pair.shape[0]
    col_count = pair.shape[1]
    hidden_width = w_out.shape[0]
    row_ids = lax.axis_index("rows") * row_count + jnp.arange(row_count, dtype=jnp.int32)
    col_ids = lax.axis_index("cols") * col_count + jnp.arange(col_count, dtype=jnp.int32)
    row_valid = (row_ids < crop_length[0]).astype(f32)
    col_valid = (col_ids < crop_length[0]).astype(f32)
    mask = (row_valid[:, None] * col_valid[None, :])[:, :, None]
    zn_full, zhat, zinv = apply_layer_norm(pair.astype(f32), gain_in)
    zn_b = zn_full.astype(to_brain_float)
    proj = jnp.dot(zn_b, w_in, preferred_element_type=f32)
    gate = jnp.dot(zn_b, w_gate, preferred_element_type=f32)
    pa_g = proj[..., 0:hidden_width]
    pa_v = proj[..., hidden_width : 2 * hidden_width]
    pb_g = proj[..., 2 * hidden_width : 3 * hidden_width]
    pb_v = proj[..., 3 * hidden_width : 4 * hidden_width]
    sig_a = jax.nn.sigmoid(pa_g)
    sig_b = jax.nn.sigmoid(pb_g)
    left = (sig_a * pa_v * mask).astype(to_brain_float)
    right = (sig_b * pb_v * mask).astype(to_brain_float)
    right_all = lax.all_gather(right, "rows", axis=0, tiled=True)
    partial_value = jnp.einsum("ikh,jkh->ijh", left, right_all, preferred_element_type=f32)
    triangle_update = lax.psum_scatter(
        partial_value.astype(jnp.bfloat16), "cols", scatter_dimension=1, tiled=True
    ).astype(jnp.float32)
    normed_input_full, centred_input, inverse_deviation = apply_layer_norm(
        triangle_update, product_norm_gain
    )
    xn_b = normed_input_full.astype(to_brain_float)
    q_out = jnp.dot(xn_b, w_out, preferred_element_type=f32)
    sig_g = jax.nn.sigmoid(gate)
    update = (sig_g * q_out).astype(to_brain_float)
    upstream = cotangent.astype(f32)
    dq_b = (upstream * sig_g).astype(to_brain_float)
    dg_b = (upstream * q_out * sig_g * (1.0 - sig_g)).astype(to_brain_float)
    local_out = jnp.einsum("ijc,ijd->cd", xn_b, dq_b, preferred_element_type=f32)
    normed_input_grad = jnp.dot(dq_b, w_out.T, preferred_element_type=f32)
    input_grad_piece = layer_norm_backward(
        normed_input_grad, product_norm_gain, centred_input, inverse_deviation
    ).astype(to_brain_float)
    dx_row = lax.all_gather(input_grad_piece, "cols", axis=1, tiled=True)
    grad_left = jnp.einsum("ijh,jkh->ikh", dx_row, right_all, preferred_element_type=f32)
    right_terms = jnp.einsum("ijh,ikh->jkh", dx_row, left, preferred_element_type=f32)
    grad_right = lax.psum_scatter(
        right_terms.astype(jnp.bfloat16), "rows", scatter_dimension=0, tiled=True
    ).astype(jnp.float32)
    dproj = jnp.concatenate(
        [
            grad_left * pa_v * mask * sig_a * (1.0 - sig_a),
            grad_left * sig_a * mask,
            grad_right * pb_v * mask * sig_b * (1.0 - sig_b),
            grad_right * sig_b * mask,
        ],
        axis=-1,
    ).astype(to_brain_float)
    local_in = jnp.einsum("ijc,ijd->cd", zn_b, dproj, preferred_element_type=f32)
    local_gate = jnp.einsum("ijc,ijd->cd", zn_b, dg_b, preferred_element_type=f32)
    grad_in, grad_gate, grad_out = lax.psum((local_in, local_gate, local_out), ("rows", "cols"))
    dzn = jnp.dot(dproj, w_in.T, preferred_element_type=f32) + jnp.dot(
        dg_b, w_gate.T, preferred_element_type=f32
    )
    pair_grad = layer_norm_backward(dzn, gain_in, zhat, zinv).astype(to_brain_float)
    return (update, pair_grad, grad_in, grad_gate, grad_out)


def solution(mesh):
    in_specs = (
        P(("groups", "rows"), "cols", None),
        P(("groups", "rows"), "cols", None),
        P("groups"),
        P(),
        P(),
        P(),
        P(),
        P(),
    )
    out_specs = (
        P(("groups", "rows"), "cols", None),
        P(("groups", "rows"), "cols", None),
        P("groups", None),
        P("groups", None),
        P("groups", None),
    )
    return jax.shard_map(
        per_device, mesh=mesh, in_specs=in_specs, out_specs=out_specs, check_vma=False
    )
```

profile of v0, /device:TPU:0, one launch (start us, length us, event | category | flops | bytes accessed | tf_op | source)
XLA Modules:
  0.0 185.4 jit_solution(13505955038577424994)
XLA Ops:
  7.2 1.0 convert_reduce_fusion.1
  9.2 0.6 copy-done.17
  10.5 7.2 %all_gather.6 = bf16[64,16,128]{2,1,0:T(8,128)(2,1)S(1)} all-gather(bf16[16,16,128]{2,1,0:T(8,128)(2,1)S(1)} %get-tuple-element.19), channel_id=1, replica_groups=mesh['groups'=2,'rows'=4,'cols'=4] {'rows'}, dimensions={0}, use_global_device_ids=true | all-gather | bytes 327680 | tf_op jit(solution)/shard_map/all_gather | solution.py:46
  17.7 0.5 copy.27
  19.1 1.3 copy.24
  20.4 21.0 %reduce-scatter.3.cloned.1.call-done = bf16[16,16,128]{2,0,1:T(8,128)(2,1)} async-done(((bf16[16,64,128]{2,0,1:T(8,128)(2,1)}), bf16[16,16,128]{2,0,1:T(8,128)(2,1)}) %reduce-scatter.3.cloned.1.call-update) | async-done | bytes 65552 | tf_op jit(solution)/shard_map/reduce_scatter | solution.py:48
  41.5 1.0 convert_reduce_fusion
  42.7 0.5 copy-done.14
  43.6 0.6 copy-done.12
  44.2 0.9 fusion.30
  45.7 13.9 %all_gather.7 = bf16[16,64,128]{2,0,1:T(8,128)(2,1)S(1)} all-gather(bf16[16,16,128]{2,0,1:T(8,128)(2,1)S(1)} %copy.26), channel_id=1, replica_groups=mesh['groups'=2,'rows'=4,'cols'=4] {'cols'}, dimensions={1}, use_global_device_ids=true | all-gather | bytes 327680 | tf_op jit(solution)/shard_map/all_gather | solution.py:66
  59.6 0.5 copy.28
  60.6 1.3 copy.32
  62.3 0.4 copy.29
  63.4 0.9 convolution_bitcast_fusion.2
  64.4 1.0 convolution_bitcast_fusion.1
  65.5 15.1 %reduce-scatter.5.cloned.1.call-done = bf16[16,16,128]{2,1,0:T(8,128)(2,1)} async-done(((bf16[64,16,128]{2,1,0:T(8,128)(2,1)}), bf16[16,16,128]{2,1,0:T(8,128)(2,1)}) %reduce-scatter.5.cloned.1.call-update) | async-done | bytes 65552 | tf_op jit(solution)/shard_map/reduce_scatter | solution.py:69
  80.6 1.0 fusion.46
  81.6 1.0 convolution_bitcast_fusion
  83.0 0.8 fusion.25
  83.8 91.8 %all-reduce.3.cloned.1.call-done = (f32[128,512]{1,0:T(8,128)}, f32[128,128]{1,0:T(8,128)}, f32[128,128]{1,0:T(8,128)}) async-done(((f32[128,512]{1,0:T(8,128)}, f32[128,128]{1,0:T(8,128)}, f32[128,128]{1,0:T(8,128)}), (f32[128,512]{1,0:T(8,128)}, f32[128,128]{1,0:T(8,128)}, f32[128,128]{1,0:T(8,128)})) %all-reduce.3.cloned.1.call-update) | async-done | bytes 393232 | tf_op jit(solution)/shard_map/psum | solution.py:83
  175.7 1.7 copy.44
  177.4 0.6 copy.45
  178.2 0.6 copy.46
  (69 shorter events, 5.2 us)
Async XLA Ops:
  7.2 2.1 %copy-start = (bf16[128,512]{1,0:T(8,128)(2,1)S(1)}, bf16[128,512]{1,0:T(8,128)(2,1)}, u32[]{:S(2)}) copy-start(bf16[128,512]{1,0:T(8,128)(2,1)} %param.12) | copy-start | bytes 393220
  7.2 1.1 copy-start.1
  7.2 34.3 %reduce-scatter.3.cloned.1.call-start = ((), (), s32[]{:S(2)}) async-start(), calls=%async_computation.2 | async-start | bytes 327680 | tf_op jit(solution)/shard_map/reduce_scatter | solution.py:48
  8.5 35.2 %copy-start.3 = (f32[16,16]{1,0:T(8,128)}, f32[16,16]{1,0:T(8,128)S(1)}, u32[]{:S(2)}) copy-start(f32[16,16]{1,0:T(8,128)S(1)} %add_rsqrt_fusion.1) | copy-start | bytes 3076
  9.1 0.7 copy-start.17
  9.8 0.6 copy-start.7
  20.4 60.2 %reduce-scatter.5.cloned.1.call-start = ((), (), s32[]{:S(2)}) async-start(), calls=%async_computation.3 | async-start | bytes 327680 | tf_op jit(solution)/shard_map/reduce_scatter | solution.py:69
  41.5 1.0 copy-start.2
  42.5 0.8 copy-start.14
  42.7 0.7 copy-start.19
  43.4 2.1 %copy-start.5 = (f32[16,16]{1,0:T(8,128)}, f32[16,16]{1,0:T(8,128)S(1)}, u32[]{:S(2)}) copy-start(f32[16,16]{1,0:T(8,128)S(1)} %add_rsqrt_fusion) | copy-start | bytes 3076
  43.4 0.8 copy-start.12
  43.4 0.8 copy-start.15
  61.9 113.8 %all-reduce.3.cloned.1.call-start = ((), (), s32[]{:S(2)}) async-start(), calls=%async_computation.4 | async-start | bytes 786432 | tf_op jit(solution)/shard_map/psum | solution.py:83
  62.3 0.7 copy-start.4
  62.3 0.9 copy-start.9
  62.8 0.7 copy-start.18
  63.4 1.0 copy-start.6
  63.4 1.0 copy-start.13
  63.4 1.0 copy-start.20
  64.4 1.0 copy-start.16
  65.4 15.3 %copy-start.8 = (f32[16,16]{1,0:T(8,128)S(1)}, f32[16,16]{1,0:T(8,128)}, u32[]{:S(2)}) copy-start(f32[16,16]{1,0:T(8,128)} %copy-done.7) | copy-start | bytes 3076
  175.7 1.7 copy-start.11
  177.4 0.9 copy-start.10
Sparse Core Ops, SparseCore 0:
  20.5 20.9 reduce-scatter.2
  62.0 18.5 reduce-scatter.4
  84.7 90.8 all-reduce.2
where the time goes:
time: 186 us; the launch traced here: 185 us
  waiting for transfers between devices  128 us (69%)
  blocking collectives  21.1 us (11%)
  between operations  14.7 us (8%)
  local copies, waits for them, and re-layouts  10.6 us (6%)
  matrix products  6.27 us (3%)
  other arithmetic  4.61 us (2%)
    psum x1, waiting for transfers between devices, per_device(): lax.psum((local_in, local_gate, local_out), ('rows', 'cols'))  91.8 us
    reduce_scatter x1, waiting for transfers between devices, per_device(): lax.psum_scatter(partial_value.astype(jnp.bfloat16), 'cols', scatter_dime...  21 us
    reduce_scatter x1, waiting for transfers between devices, per_device(): lax.psum_scatter(right_terms.astype(jnp.bfloat16), 'rows', scatter_dimens...  15.1 us
    all_gather x1, blocking collectives, per_device(): dx_row = lax.all_gather(input_grad_piece, 'cols', axis=1, tiled=True)  13.9 us
    all_gather x1, blocking collectives, per_device(): right_all = lax.all_gather(right, 'rows', axis=0, tiled=True)  7.22 us
    unnamed x45, local copies, waits for them, and re-layouts  6.05 us
  transfers between devices with their start and end apart: 3, of which 3 were waited for; matrix products, arithmetic and copies ran while one was open for 2% of the time, Pallas kernels for 0%

commit v1 on v0

--- a/solution.py
+++ b/solution.py
@@ -1,6 +1,10 @@
+import functools
+
 import jax
 import jax.numpy as jnp
 from jax import lax
+from jax.experimental import pallas as pl
+from jax.experimental.pallas import tpu as pltpu
 from jax.sharding import PartitionSpec as P
 
 
@@ -88,6 +92,352 @@
     return (update, pair_grad, grad_in, grad_gate, grad_out)
 
 
+MESH = pl.DeviceIdType.MESH
+
+
+def last_mean(values):
+    return jnp.mean(values, axis=-1, keepdims=True)
+
+
+def dot_t(lhs, rhs):
+    return lax.dot_general(lhs, rhs, (((1,), (1,)), ((), ())), preferred_element_type=jnp.float32)
+
+
+def fused_kernel(
+    n,
+    crop_ref,
+    pair_ref,
+    cot_ref,
+    gain_in_ref,
+    w_in_ref,
+    w_gate_ref,
+    gain_x_ref,
+    w_out_ref,
+    update_ref,
+    pair_grad_ref,
+    grad_in_ref,
+    grad_gate_ref,
+    grad_out_ref,
+    b_all,
+    x_send,
+    x_recv,
+    dx_all,
+    db_send,
+    db_recv,
+    w_part,
+    w_recv,
+    w_all,
+    left_f,
+    right_f,
+    dx_f,
+    da_f,
+    proj_ref,
+    zn_ref,
+    b_ss,
+    b_rs,
+    x_ss,
+    x_rs,
+    dx_ss,
+    dx_rs,
+    db_ss,
+    db_rs,
+    ws_ss,
+    ws_rs,
+    wg_ss,
+    wg_rs,
+):
+    f32, bf16 = jnp.float32, jnp.bfloat16
+    blk, _, width = pair_ref.shape
+    size = blk * blk
+    total = n * n
+    share = 2 * width // total
+    row = lax.axis_index("rows")
+    col = lax.axis_index("cols")
+    me = row * n + col
+
+    def peer(step):
+        other = lax.rem(me + step, total)
+        return other, {"rows": lax.div(other, n), "cols": lax.rem(other, n)}
+
+    barrier = pltpu.get_barrier_semaphore()
+    for step in range(1, total):
+        _, target = peer(step)
+        pl.semaphore_signal(barrier, inc=1, device_id=target, device_id_type=MESH)
+
+    def b_copy(slot, other):
+        return pltpu.make_async_remote_copy(
+            b_all.at[slot], b_all.at[slot], b_ss.at[other], b_rs.at[slot],
+            device_id={"rows": other}, device_id_type=MESH)
+
+    def x_copy(block, slot):
+        return pltpu.make_async_remote_copy(
+            x_send.at[block], x_recv.at[slot], x_ss.at[block], x_rs.at[slot],
+            device_id={"cols": block}, device_id_type=MESH)
+
+    def dx_copy(slot, other):
+        return pltpu.make_async_remote_copy(
+            dx_all.at[slot], dx_all.at[slot], dx_ss.at[other], dx_rs.at[slot],
+            device_id={"cols": other}, device_id_type=MESH)
+
+    def db_copy(block, slot):
+        return pltpu.make_async_remote_copy(
+            db_send.at[block], db_recv.at[slot], db_ss.at[block], db_rs.at[slot],
+            device_id={"rows": block}, device_id_type=MESH)
+
+    def ws_copy(group, other, target, slot):
+        return pltpu.make_async_remote_copy(
+            w_part.at[group, other], w_recv.at[group, slot],
+            ws_ss.at[group, other], ws_rs.at[group, slot],
+            device_id=target, device_id_type=MESH)
+
+    def wg_copy(group, other, target, slot):
+        return pltpu.make_async_remote_copy(
+            w_all.at[group, slot], w_all.at[group, slot],
+            wg_ss.at[group, other], wg_rs.at[group, slot],
+            device_id=target, device_id_type=MESH)
+
+    def scatter_weights(group, first, second):
+        half = total // 2
+        w_part[group, 0:half] = first.astype(bf16).reshape(half, share, width)
+        w_part[group, half:total] = second.astype(bf16).reshape(half, share, width)
+
+        @pl.loop(1, total)
+        def _(step):
+            other, target = peer(step)
+            ws_copy(group, other, target, me).start()
+
+    def gather_weights(group):
+        w_recv[group, me] = w_part[group, me]
+
+        @pl.loop(1, total)
+        def _(step):
+            other, target = peer(step)
+            ws_copy(group, other, target, other).wait_recv()
+
+        summed = jnp.sum(w_recv[group].astype(f32), axis=0)
+        w_all[group, me] = summed.astype(bf16)
+
+        @pl.loop(1, total)
+        def _(step):
+            other, target = peer(step)
+            wg_copy(group, other, target, me).start()
+
+    def finish_weights(group):
+        @pl.loop(1, total)
+        def _(step):
+            other, target = peer(step)
+            wg_copy(group, other, target, other).wait_recv()
+
+        whole = w_all[group].reshape(2 * width, width).astype(f32)
+        return whole[:width], whole[width:]
+
+    gain_in = gain_in_ref[...]
+    pair = pair_ref[...].reshape(size, width).astype(f32)
+    centre = pair - last_mean(pair)
+    zinv = lax.rsqrt(last_mean(centre * centre) + 1e-05)
+    zhat = centre * zinv
+    zn_f = zhat * gain_in
+    zn = zn_f.astype(bf16)
+    zn_ref[...] = zn_f.T.astype(bf16)
+    crop = crop_ref[0]
+    place = lax.broadcasted_iota(jnp.int32, (size, width), 0)
+    row_ids = row * blk + lax.div(place, blk)
+    col_ids = col * blk + lax.rem(place, blk)
+    mask = jnp.where((row_ids < crop) & (col_ids < crop), 1.0, 0.0).astype(f32)
+    proj_ref[...] = jnp.dot(zn, w_in_ref[...], preferred_element_type=f32)
+
+    sig_b = jax.nn.sigmoid(proj_ref[:, 2 * width : 3 * width])
+    right = (sig_b * proj_ref[:, 3 * width : 4 * width] * mask).astype(bf16)
+    b_all[row] = right.reshape(blk, blk, width)
+
+    pl.semaphore_wait(barrier, total - 1)
+    for step in range(1, n):
+        b_copy(row, lax.rem(row + step, n)).start()
+
+    sig_a = jax.nn.sigmoid(proj_ref[:, 0:width])
+    left = (sig_a * proj_ref[:, width : 2 * width] * mask).astype(bf16).astype(f32)
+    left_f[...] = left.reshape(blk, blk, width)
+    sig_g = jax.nn.sigmoid(jnp.dot(zn, w_gate_ref[...], preferred_element_type=f32))
+
+    for step in range(n):
+        block = lax.rem(row + step, n)
+        if step > 0:
+            b_copy(block, block).wait_recv()
+        right_f[...] = jnp.swapaxes(b_all[block].astype(f32), 0, 1)
+
+        @pl.loop(0, blk)
+        def _(i):
+            line = left_f[i]
+            x_send[block, i] = jnp.sum(line[:, None, :] * right_f[...], axis=0).astype(bf16)
+
+        @pl.when(block != col)
+        def _():
+            x_copy(block, col).start()
+
+    x = x_send[col].astype(f32)
+    for step in range(1, n):
+        other = lax.rem(col + step, n)
+        x_copy(other, other).wait_recv()
+        x = x + x_recv[other].astype(f32)
+    x = x.reshape(size, width)
+
+    gain_x = gain_x_ref[...]
+    w_out = w_out_ref[...]
+    cot = cot_ref[...].reshape(size, width).astype(f32)
+    centre = x - last_mean(x)
+    xinv = lax.rsqrt(last_mean(centre * centre) + 1e-05)
+    xhat = centre * xinv
+    xn_f = xhat * gain_x
+    dq = (cot * sig_g).astype(bf16)
+    scaled = dot_t(dq, w_out) * gain_x
+    dx = xinv * (scaled - last_mean(scaled) - xhat * last_mean(scaled * xhat))
+    dx_all[col] = dx.astype(bf16).reshape(blk, blk, width)
+    for step in range(1, n):
+        dx_copy(col, lax.rem(col + step, n)).start()
+    q_out = jnp.dot(xn_f.astype(bf16), w_out, preferred_element_type=f32)
+    update_ref[...] = (sig_g * q_out).astype(bf16).reshape(blk, blk, width)
+    dg = (cot * q_out * sig_g * (1.0 - sig_g)).astype(bf16)
+    zn_t = zn_ref[...]
+    scatter_weights(
+        0,
+        jnp.dot(zn_t, dg, preferred_element_type=f32),
+        jnp.dot(xn_f.T.astype(bf16), dq, preferred_element_type=f32),
+    )
+
+    da_f[...] = jnp.zeros_like(da_f)
+    for step in range(n):
+        block = lax.rem(col + step, n)
+        if step > 0:
+            dx_copy(block, block).wait_recv()
+        dx_f[...] = dx_all[block].astype(f32)
+        right_f[...] = b_all[block].astype(f32)
+
+        def over_i(i, db):
+            line = dx_f[i][:, None, :]
+            da_f[i] += jnp.sum(line * right_f[...], axis=0)
+            return db + line * left_f[i][None]
+
+        db = lax.fori_loop(0, blk, over_i, jnp.zeros((blk, blk, width), f32))
+        db_send[block] = db.astype(bf16)
+
+        @pl.when(block != row)
+        def _():
+            db_copy(block, row).start()
+
+    da = da_f[...].reshape(size, width)
+    pa_v = proj_ref[:, width : 2 * width]
+    d_ag = (da * pa_v * mask * sig_a * (1.0 - sig_a)).astype(bf16)
+    d_av = (da * sig_a * mask).astype(bf16)
+    scatter_weights(
+        1,
+        jnp.dot(zn_t, d_ag, preferred_element_type=f32),
+        jnp.dot(zn_t, d_av, preferred_element_type=f32),
+    )
+    dzn = dot_t(dg, w_gate_ref[...]) + dot_t(d_ag, w_in_ref[:, 0:width])
+    dzn = dzn + dot_t(d_av, w_in_ref[:, width : 2 * width])
+    gather_weights(0)
+
+    db = db_send[row].astype(f32)
+    for step in range(1, n):
+        other = lax.rem(row + step, n)
+        db_copy(other, other).wait_recv()
+        db = db + db_recv[other].astype(f32)
+    db = db.reshape(size, width)
+    pb_v = proj_ref[:, 3 * width : 4 * width]
+    d_bg = (db * pb_v * mask * sig_b * (1.0 - sig_b)).astype(bf16)
+    d_bv = (db * sig_b * mask).astype(bf16)
+    scatter_weights(
+        2,
+        jnp.dot(zn_t, d_bg, preferred_element_type=f32),
+        jnp.dot(zn_t, d_bv, preferred_element_type=f32),
+    )
+    gather_weights(1)
+    dzn = dzn + dot_t(d_bg, w_in_ref[:, 2 * width : 3 * width])
+    dzn = dzn + dot_t(d_bv, w_in_ref[:, 3 * width : 4 * width])
+    scaled = dzn * gain_in
+    pair_grad = zinv * (scaled - last_mean(scaled) - zhat * last_mean(scaled * zhat))
+    pair_grad_ref[...] = pair_grad.astype(bf16).reshape(blk, blk, width)
+    gather_weights(2)
+    grad_gate_ref[...], grad_out_ref[...] = finish_weights(0)
+    grad_in_ref[:, 0:width], grad_in_ref[:, width : 2 * width] = finish_weights(1)
+    grad_in_ref[:, 2 * width : 3 * width], grad_in_ref[:, 3 * width : 4 * width] = finish_weights(2)
+
+    for step in range(1, n):
+        b_copy(row, lax.rem(row + step, n)).wait_send()
+        dx_copy(col, lax.rem(col + step, n)).wait_send()
+        x_copy(lax.rem(col + step, n), col).wait_send()
+        db_copy(lax.rem(row + step, n), row).wait_send()
+
+    @pl.loop(1, total)
+    def _(step):
+        other, target = peer(step)
+        for group in range(3):
+            ws_copy(group, other, target, me).wait_send()
+            wg_copy(group, other, target, me).wait_send()
+
+
+def fused_plan(n, pair, cotangent, crop_length, gain_in, w_in, w_gate, product_norm_gain, w_out):
+    blk, _, width = pair.shape
+    total = n * n
+    share = 2 * width // total
+    f32, bf16 = jnp.float32, jnp.bfloat16
+    shape = jax.ShapeDtypeStruct
+    blocks = (n, blk, blk, width)
+    shares = (3, total, share, width)
+    dma = pltpu.SemaphoreType.DMA
+    vmem = pl.BlockSpec(memory_space=pltpu.VMEM)
+    return pl.pallas_call(
+        functools.partial(fused_kernel, n),
+        out_shape=(
+            shape(pair.shape, bf16),
+            shape(pair.shape, bf16),
+            shape(w_in.shape, f32),
+            shape(w_gate.shape, f32),
+            shape(w_out.shape, f32),
+        ),
+        in_specs=[pl.BlockSpec(memory_space=pltpu.SMEM)] + [vmem] * 7,
+        out_specs=(vmem,) * 5,
+        scratch_shapes=[
+            pltpu.VMEM(blocks, bf16),
+            pltpu.VMEM(blocks, bf16),
+            pltpu.VMEM(blocks, bf16),
+            pltpu.VMEM(blocks, bf16),
+            pltpu.VMEM(blocks, bf16),
+            pltpu.VMEM(blocks, bf16),
+            pltpu.VMEM(shares, bf16),
+            pltpu.VMEM(shares, bf16),
+            pltpu.VMEM(shares, bf16),
+            pltpu.VMEM(blocks[1:], f32),
+            pltpu.VMEM(blocks[1:], f32),
+            pltpu.VMEM(blocks[1:], f32),
+            pltpu.VMEM(blocks[1:], f32),
+            pltpu.VMEM((blk * blk, 4 * width), f32),
+            pltpu.VMEM((width, blk * blk), bf16),
+        ]
+        + [dma((n,))] * 8
+        + [dma((3, total))] * 4,
+        compiler_params=pltpu.CompilerParams(
+            collective_id=0, has_side_effects=True, vmem_limit_bytes=40 * 1024 * 1024
+        ),
+    )(
+        crop_length,
+        pair,
+        cotangent,
+        gain_in.reshape(1, width),
+        w_in,
+        w_gate,
+        product_norm_gain.reshape(1, width),
+        w_out,
+    )
+
+
+def choose_plan(n_rows, n_cols, pair, cotangent, crop_length, gain_in, w_in, w_gate, product_norm_gain, w_out):
+    args = (pair, cotangent, crop_length, gain_in, w_in, w_gate, product_norm_gain, w_out)
+    square = n_rows == n_cols and pair.shape[0] == pair.shape[1] == 16
+    even = w_in.shape == (128, 512) and 256 % (16 * n_rows * n_cols) == 0
+    return fused_plan(n_rows, *args) if square and even else per_device(*args)
+
+
 def solution(mesh):
     in_specs = (
         P(("groups", "rows"), "cols", None),
@@ -107,5 +457,5 @@
         P("groups", None),
     )
     return jax.shard_map(
-        per_device, mesh=mesh, in_specs=in_specs, out_specs=out_specs, check_vma=False
-    )
+        functools.partial(choose_plan, mesh.shape["rows"], mesh.shape["cols"]), mesh=mesh, in_specs=in_specs, out_specs=out_specs, check_vma=False
+    )

time: 186 us -> 54 us (0.29)
  waiting for transfers between devices: 128 us -> 0 us
  Pallas kernels: 0 us -> 44.4 us
  blocking collectives: 21.1 us -> 0 us
  between operations: 14.7 us -> 1.31 us
  matrix products: 6.27 us -> 0 us
  other arithmetic: 4.61 us -> 0 us
  local copies, waits for them, and re-layouts: 10.6 us -> 7.97 us
    psum x1 -> x0, waiting for transfers between devices: 91.8 us -> none  [per_device(): lax.psum((local_in, local_gate, local_out), ('rows', 'cols'))]
    pallas_call x0 -> x1, Pallas kernels: none -> 44.4 us  [fused_plan(): pl.pallas_call(functools.partial(fused_kernel, n), out_shape=(shape(pair....]
    reduce_scatter x2 -> x0, waiting for transfers between devices: 36.1 us -> none  [the longest x1 21 us: per_device(): lax.psum_scatter(partial_value.astype(jnp.bfloat16), 'cols', scatter_dime...]
    all_gather x2 -> x0, blocking collectives: 21.1 us -> none  [the longest x1 13.9 us: per_device(): dx_row = lax.all_gather(input_grad_piece, 'cols', axis=1, tiled=True)]
    dot_general x12 -> x0, matrix products: 6.27 us -> none  [the longest x1 1.03 us: per_device(): jnp.einsum('ijc,ijd->cd', zn_b, dproj, preferred_element_type=f32)]
    reduce_sum x4 -> x0, other arithmetic: 2.37 us -> none  [the longest x2 1.99 us: apply_layer_norm(): centre = values - jnp.mean(values, axis=-1, keepdims=True)]
    unnamed x45 -> x19, local copies, waits for them, and re-layouts: 6.05 us -> 7.97 us
  transfers between devices with their start and end apart: 3 -> 0, of which waited for: 3 -> 0; matrix products, arithmetic and copies ran while one was open for 2% -> 0% of each run, Pallas kernels for 0% -> 0%
where the time goes in v1:
time: 54 us; the launch traced here: 53.7 us
  Pallas kernels  44.4 us (82%)
  local copies, waits for them, and re-layouts  7.97 us (15%)
  between operations  1.31 us (2%)
    pallas_call x1, Pallas kernels, fused_plan(): pl.pallas_call(functools.partial(fused_kernel, n), out_shape=(shape(pair....  44.4 us
    unnamed x19, local copies, waits for them, and re-layouts  7.97 us

profile of v1, /device:TPU:0, one launch (start us, length us, event | category | flops | bytes accessed | tf_op | source)
XLA Modules:
  0.0 53.7 jit_solution(549885447159590916)
XLA Ops:
  1.3 0.0 copy-start.5
  1.3 0.0 copy-start.6
  1.3 0.6 %copy-done.5 = f32[128]{0:T(128)S(1)} copy-done((f32[128]{0:T(128)S(1)}, f32[128]{0:T(128)}, u32[]{:S(2)}) %copy-start.5) | copy-done | bytes 536
  1.9 0.0 copy-done.6
  2.0 0.0 copy-start
  2.0 0.9 %copy-done = bf16[128,512]{1,0:T(8,128)(2,1)S(1)} copy-done((bf16[128,512]{1,0:T(8,128)(2,1)S(1)}, bf16[128,512]{1,0:T(8,128)(2,1)}, u32[]{:S(2)}) %copy-start) | copy-done | bytes 131096
  2.9 0.0 copy-start.1
  2.9 0.8 %copy-done.1 = bf16[16,16,128]{2,1,0:T(8,128)(2,1)S(1)} copy-done((bf16[16,16,128]{2,1,0:T(8,128)(2,1)S(1)}, bf16[16,16,128]{2,1,0:T(8,128)(2,1)}, u32[]{:S(2)}) %copy-start.1) | copy-done | bytes 65560
  3.7 0.0 copy-start.2
  3.7 0.8 %copy-done.2 = bf16[16,16,128]{2,1,0:T(8,128)(2,1)S(1)} copy-done((bf16[16,16,128]{2,1,0:T(8,128)(2,1)S(1)}, bf16[16,16,128]{2,1,0:T(8,128)(2,1)}, u32[]{:S(2)}) %copy-start.2) | copy-done | bytes 65560
  4.5 0.0 copy-start.3
  4.5 0.8 %copy-done.3 = bf16[128,128]{1,0:T(8,128)(2,1)S(1)} copy-done((bf16[128,128]{1,0:T(8,128)(2,1)S(1)}, bf16[128,128]{1,0:T(8,128)(2,1)}, u32[]{:S(2)}) %copy-start.3) | copy-done | bytes 32792
  5.3 0.0 copy-start.4
  5.3 0.8 %copy-done.4 = bf16[128,128]{1,0:T(8,128)(2,1)S(1)} copy-done((bf16[128,128]{1,0:T(8,128)(2,1)S(1)}, bf16[128,128]{1,0:T(8,128)(2,1)}, u32[]{:S(2)}) %copy-start.4) | copy-done | bytes 32792
  6.1 44.4 %shard_map.119 = (bf16[16,16,128]{2,1,0:T(8,128)(2,1)S(1)}, bf16[16,16,128]{2,1,0:T(8,128)(2,1)S(1)}, f32[128,512]{1,0:T(8,128)S(1)}, f32[128,128]{1,0:T(8,128)S(1)}, f32[128,128]{1,0:T(8,128)S(1)}) custom-call(s32[1]{0:T(128)S(6)} %copy.18.crop_ref, bf16[16,16,128]{2,1,0:T(8,128)(2,1)S(1)} %copy-done.1, bf16[16,16,128]{2,1,0:T(8,128)(2,1)S(1)} %copy-done.2, ...), custom_call_target="tpu_custom_call" | custom-call | tf_op jit(solution)/shard_map/pallas_call | solution.py:389
  50.4 0.6 %copy.19 = bf16[16,16,128]{2,1,0:T(8,128)(2,1)} copy(bf16[16,16,128]{2,1,0:T(8,128)(2,1)S(1)} %get-tuple-element.10) | data formatting | bytes 131072
  51.1 0.6 %copy.20 = bf16[16,16,128]{2,1,0:T(8,128)(2,1)} copy(bf16[16,16,128]{2,1,0:T(8,128)(2,1)S(1)} %get-tuple-element.11) | data formatting | bytes 131072
  51.7 0.7 %copy.21 = f32[128,512]{1,0:T(8,128)} copy(f32[128,512]{1,0:T(8,128)S(1)} %get-tuple-element.12) | data formatting | bytes 524288
  52.4 0.6 %copy.22 = f32[128,128]{1,0:T(8,128)} copy(f32[128,128]{1,0:T(8,128)S(1)} %get-tuple-element.13) | data formatting | bytes 131072
  53.0 0.6 %copy.23 = f32[128,128]{1,0:T(8,128)} copy(f32[128,128]{1,0:T(8,128)S(1)} %get-tuple-element.14) | data formatting | bytes 131072
Async XLA Ops:
  1.3 0.7 %copy-start.5 = (f32[128]{0:T(128)S(1)}, f32[128]{0:T(128)}, u32[]{:S(2)}) copy-start(f32[128]{0:T(128)} %param.11) | copy-start | bytes 1540
  1.3 0.7 %copy-start.6 = (f32[128]{0:T(128)S(1)}, f32[128]{0:T(128)}, u32[]{:S(2)}) copy-start(f32[128]{0:T(128)} %param.14) | copy-start | bytes 1540
  2.0 0.9 %copy-start = (bf16[128,512]{1,0:T(8,128)(2,1)S(1)}, bf16[128,512]{1,0:T(8,128)(2,1)}, u32[]{:S(2)}) copy-start(bf16[128,512]{1,0:T(8,128)(2,1)} %w_in_ref.1) | copy-start | bytes 393220
  2.9 0.8 %copy-start.1 = (bf16[16,16,128]{2,1,0:T(8,128)(2,1)S(1)}, bf16[16,16,128]{2,1,0:T(8,128)(2,1)}, u32[]{:S(2)}) copy-start(bf16[16,16,128]{2,1,0:T(8,128)(2,1)} %pair_ref.1) | copy-start | bytes 196612
  3.7 0.8 %copy-start.2 = (bf16[16,16,128]{2,1,0:T(8,128)(2,1)S(1)}, bf16[16,16,128]{2,1,0:T(8,128)(2,1)}, u32[]{:S(2)}) copy-start(bf16[16,16,128]{2,1,0:T(8,128)(2,1)} %cot_ref.1) | copy-start | bytes 196612
  4.5 0.8 %copy-start.3 = (bf16[128,128]{1,0:T(8,128)(2,1)S(1)}, bf16[128,128]{1,0:T(8,128)(2,1)}, u32[]{:S(2)}) copy-start(bf16[128,128]{1,0:T(8,128)(2,1)} %w_gate_ref.1) | copy-start | bytes 98308
  5.3 0.8 %copy-start.4 = (bf16[128,128]{1,0:T(8,128)(2,1)S(1)}, bf16[128,128]{1,0:T(8,128)(2,1)}, u32[]{:S(2)}) copy-start(bf16[128,128]{1,0:T(8,128)(2,1)} %w_out_ref.1) | copy-start | bytes 98308

commit v2 on v1

--- a/solution.py
+++ b/solution.py
@@ -92,6 +92,7 @@
     return (update, pair_grad, grad_in, grad_gate, grad_out)
 
 
+VMEM_GRANT = 63 * 1024 * 1024
 MESH = pl.DeviceIdType.MESH
 
 
@@ -106,48 +107,59 @@
 def fused_kernel(
     n,
     crop_ref,
-    pair_ref,
+    pair_hbm,
+    cot_hbm,
+    gain_in_hbm,
+    w_in_hbm,
+    w_gate_hbm,
+    gain_x_hbm,
+    w_out_hbm,
+    update_ref,
+    pair_grad_ref,
+    grad_in_ref,
+    grad_gate_ref,
+    grad_out_ref,
+    pair_all,
+    b_all,
+    x_send,
+    x_recv,
+    dx_all,
+    db_send,
+    db_recv,
+    w0_part,
+    w0_recv,
+    w1_part,
+    w1_recv,
+    w_all,
+    zn_all,
+    slope_g,
+    slope_v,
+    b_sums,
     cot_ref,
     gain_in_ref,
     w_in_ref,
     w_gate_ref,
     gain_x_ref,
     w_out_ref,
-    update_ref,
-    pair_grad_ref,
-    grad_in_ref,
-    grad_gate_ref,
-    grad_out_ref,
-    b_all,
-    x_send,
-    x_recv,
-    dx_all,
-    db_send,
-    db_recv,
-    w_part,
-    w_recv,
-    w_all,
     left_f,
     right_f,
     dx_f,
     da_f,
     proj_ref,
-    zn_ref,
-    b_ss,
-    b_rs,
+    pair_ss,
+    pair_rs,
     x_ss,
     x_rs,
     dx_ss,
     dx_rs,
     db_ss,
     db_rs,
-    ws_ss,
-    ws_rs,
-    wg_ss,
-    wg_rs,
+    w_ss,
+    w_rs,
+    in_sem,
 ):
     f32, bf16 = jnp.float32, jnp.bfloat16
-    blk, _, width = pair_ref.shape
+    blk, _, width = pair_hbm.shape
     size = blk * blk
     total = n * n
     share = 2 * width // total
@@ -159,14 +171,37 @@
         other = lax.rem(me + step, total)
         return other, {"rows": lax.div(other, n), "cols": lax.rem(other, n)}
 
+    def nearest(place):
+        for step in range(0, n, 2):
+            base = lax.rem(place + step, n)
+            yield base
+            yield base + 1 - 2 * lax.rem(base, 2)
+
+    near = list(nearest(row))
+
+    fetches = [
+        pltpu.make_async_copy(source, target, in_sem.at[at])
+        for at, (source, target) in enumerate([
+            (pair_hbm, pair_all.at[row]),
+            (gain_in_hbm, gain_in_ref),
+            (w_in_hbm, w_in_ref),
+            (w_gate_hbm, w_gate_ref),
+            (cot_hbm, cot_ref),
+            (w_out_hbm, w_out_ref),
+            (gain_x_hbm, gain_x_ref),
+        ])
+    ]
+    for fetch in fetches:
+        fetch.start()
+
     barrier = pltpu.get_barrier_semaphore()
     for step in range(1, total):
         _, target = peer(step)
         pl.semaphore_signal(barrier, inc=1, device_id=target, device_id_type=MESH)
 
-    def b_copy(slot, other):
+    def pair_copy(slot, other):
         return pltpu.make_async_remote_copy(
-            b_all.at[slot], b_all.at[slot], b_ss.at[other], b_rs.at[slot],
+            pair_all.at[slot], pair_all.at[slot], pair_ss.at[other], pair_rs.at[slot],
             device_id={"rows": other}, device_id_type=MESH)
 
     def x_copy(block, slot):
@@ -184,85 +219,67 @@
             db_send.at[block], db_recv.at[slot], db_ss.at[block], db_rs.at[slot],
             device_id={"rows": block}, device_id_type=MESH)
 
-    def ws_copy(group, other, target, slot):
+    def w_copy(stage, source, target, device):
         return pltpu.make_async_remote_copy(
-            w_part.at[group, other], w_recv.at[group, slot],
-            ws_ss.at[group, other], ws_rs.at[group, slot],
-            device_id=target, device_id_type=MESH)
-
-    def wg_copy(group, other, target, slot):
-        return pltpu.make_async_remote_copy(
-            w_all.at[group, slot], w_all.at[group, slot],
-            wg_ss.at[group, other], wg_rs.at[group, slot],
-            device_id=target, device_id_type=MESH)
-
-    def scatter_weights(group, first, second):
-        half = total // 2
-        w_part[group, 0:half] = first.astype(bf16).reshape(half, share, width)
-        w_part[group, half:total] = second.astype(bf16).reshape(half, share, width)
-
-        @pl.loop(1, total)
-        def _(step):
+            source, target, w_ss.at[stage], w_rs.at[stage],
+            device_id=device, device_id_type=MESH)
+
+    def w_stage(stage, buffer):
+        piece = buffer.at[pl.ds(0, total - 1)]
+        return w_copy(stage, piece, piece, peer(1)[1])
+
+    def scatter_weights(stage, outgoing, arriving):
+        for step in range(1, total):
             other, target = peer(step)
-            ws_copy(group, other, target, me).start()
-
-    def gather_weights(group):
-        w_recv[group, me] = w_part[group, me]
-
-        @pl.loop(1, total)
-        def _(step):
-            other, target = peer(step)
-            ws_copy(group, other, target, other).wait_recv()
-
-        summed = jnp.sum(w_recv[group].astype(f32), axis=0)
-        w_all[group, me] = summed.astype(bf16)
-
-        @pl.loop(1, total)
-        def _(step):
-            other, target = peer(step)
-            wg_copy(group, other, target, me).start()
-
-    def finish_weights(group):
-        @pl.loop(1, total)
-        def _(step):
-            other, target = peer(step)
-            wg_copy(group, other, target, other).wait_recv()
-
-        whole = w_all[group].reshape(2 * width, width).astype(f32)
-        return whole[:width], whole[width:]
-
-    gain_in = gain_in_ref[...]
-    pair = pair_ref[...].reshape(size, width).astype(f32)
-    centre = pair - last_mean(pair)
-    zinv = lax.rsqrt(last_mean(centre * centre) + 1e-05)
-    zhat = centre * zinv
-    zn_f = zhat * gain_in
-    zn = zn_f.astype(bf16)
-    zn_ref[...] = zn_f.T.astype(bf16)
+            w_copy(stage, outgoing.at[other], arriving.at[me], target).start()
+        arriving[me] = outgoing[me]
+
     crop = crop_ref[0]
     place = lax.broadcasted_iota(jnp.int32, (size, width), 0)
-    row_ids = row * blk + lax.div(place, blk)
-    col_ids = col * blk + lax.rem(place, blk)
-    mask = jnp.where((row_ids < crop) & (col_ids < crop), 1.0, 0.0).astype(f32)
-    proj_ref[...] = jnp.dot(zn, w_in_ref[...], preferred_element_type=f32)
-
-    sig_b = jax.nn.sigmoid(proj_ref[:, 2 * width : 3 * width])
-    right = (sig_b * proj_ref[:, 3 * width : 4 * width] * mask).astype(bf16)
-    b_all[row] = right.reshape(blk, blk, width)
-
+    row_ids = lax.div(place, blk)
+    col_ok = col * blk + lax.rem(place, blk) < crop
+
+    def mask_of(block):
+        return jnp.where((block * blk + row_ids < crop) & col_ok, 1.0, 0.0).astype(f32)
+
+    def normed(block):
+        pair = pair_all[block].reshape(size, width).astype(f32)
+        centre = pair - last_mean(pair)
+        zinv = lax.rsqrt(last_mean(centre * centre) + 1e-05)
+        return centre * zinv, zinv
+
+    def prepare(block):
+        zhat, _ = normed(block)
+        zn_f = zhat * gain_in_ref[...]
+        zn = zn_f.astype(bf16)
+        mask = mask_of(block)
+        pb = jnp.dot(zn, w_in_ref[:, 2 * width : 4 * width], preferred_element_type=f32)
+        gated = jax.nn.sigmoid(pb[:, :width]) * mask
+        right = (gated * pb[:, width:]).astype(bf16)
+        b_all[block] = right.reshape(blk, blk, width)
+        zn_all[block] = zn_f.T.astype(bf16)
+        slope_v[block] = gated
+        slope_g[block] = gated * pb[:, width:] * (1.0 - jax.nn.sigmoid(pb[:, :width]))
+        return zn
+
+    for fetch in fetches[:4]:
+        fetch.wait()
+    zn = prepare(row)
     pl.semaphore_wait(barrier, total - 1)
-    for step in range(1, n):
-        b_copy(row, lax.rem(row + step, n)).start()
-
+    for other in near[1:]:
+        pair_copy(row, other).start()
+
+    mask = mask_of(row)
+    proj_ref[...] = jnp.dot(zn, w_in_ref[:, 0 : 2 * width], preferred_element_type=f32)
     sig_a = jax.nn.sigmoid(proj_ref[:, 0:width])
     left = (sig_a * proj_ref[:, width : 2 * width] * mask).astype(bf16).astype(f32)
     left_f[...] = left.reshape(blk, blk, width)
     sig_g = jax.nn.sigmoid(jnp.dot(zn, w_gate_ref[...], preferred_element_type=f32))
 
-    for step in range(n):
-        block = lax.rem(row + step, n)
+    for step, block in enumerate(near):
         if step > 0:
-            b_copy(block, block).wait_recv()
+            pair_copy(block, block).wait_recv()
+            prepare(block)
         right_f[...] = jnp.swapaxes(b_all[block].astype(f32), 0, 1)
 
         @pl.loop(0, blk)
@@ -281,6 +298,8 @@
         x = x + x_recv[other].astype(f32)
     x = x.reshape(size, width)
 
+    for fetch in fetches[4:]:
+        fetch.wait()
     gain_x = gain_x_ref[...]
     w_out = w_out_ref[...]
     cot = cot_ref[...].reshape(size, width).astype(f32)
@@ -297,14 +316,17 @@
     q_out = jnp.dot(xn_f.astype(bf16), w_out, preferred_element_type=f32)
     update_ref[...] = (sig_g * q_out).astype(bf16).reshape(blk, blk, width)
     dg = (cot * q_out * sig_g * (1.0 - sig_g)).astype(bf16)
-    zn_t = zn_ref[...]
-    scatter_weights(
-        0,
-        jnp.dot(zn_t, dg, preferred_element_type=f32),
-        jnp.dot(xn_f.T.astype(bf16), dq, preferred_element_type=f32),
-    )
+    zn_t = zn_all[row]
+    half = total // 2
+    w0_part[0:half] = (
+        jnp.dot(zn_t, dg, preferred_element_type=f32).astype(bf16).reshape(half, share, width))
+    w0_part[half:total] = (
+        jnp.dot(xn_f.T.astype(bf16), dq, preferred_element_type=f32)
+        .astype(bf16).reshape(half, share, width))
+    scatter_weights(0, w0_part, w0_recv)
 
     da_f[...] = jnp.zeros_like(da_f)
+    b_sums[...] = jnp.zeros_like(b_sums)
     for step in range(n):
         block = lax.rem(col + step, n)
         if step > 0:
@@ -324,56 +346,78 @@
         def _():
             db_copy(block, row).start()
 
+        terms = db.reshape(size, width)
+        zn_block = zn_all[block]
+        b_sums[0] += jnp.dot(
+            zn_block, (terms * slope_g[block]).astype(bf16), preferred_element_type=f32)
+        b_sums[1] += jnp.dot(
+            zn_block, (terms * slope_v[block]).astype(bf16), preferred_element_type=f32)
+
     da = da_f[...].reshape(size, width)
     pa_v = proj_ref[:, width : 2 * width]
     d_ag = (da * pa_v * mask * sig_a * (1.0 - sig_a)).astype(bf16)
     d_av = (da * sig_a * mask).astype(bf16)
-    scatter_weights(
-        1,
+    quarter = total // 4
+    sums = (
         jnp.dot(zn_t, d_ag, preferred_element_type=f32),
         jnp.dot(zn_t, d_av, preferred_element_type=f32),
-    )
+        b_sums[0],
+        b_sums[1],
+    )
+    for at, term in enumerate(sums):
+        w1_part[at * quarter : (at + 1) * quarter] = (
+            term.astype(bf16).reshape(quarter, 2 * share, width))
+    scatter_weights(1, w1_part, w1_recv)
     dzn = dot_t(dg, w_gate_ref[...]) + dot_t(d_ag, w_in_ref[:, 0:width])
     dzn = dzn + dot_t(d_av, w_in_ref[:, width : 2 * width])
-    gather_weights(0)
+    w_stage(0, w0_recv).wait_recv()
+    w_all[me, 0:share] = jnp.sum(w0_recv[...].astype(f32), axis=0).astype(bf16)
+    w_stage(1, w1_recv).wait_recv()
+    w_all[me, share : 3 * share] = jnp.sum(w1_recv[...].astype(f32), axis=0).astype(bf16)
+    for step in range(1, total):
+        _, target = peer(step)
+        w_copy(2, w_all.at[me], w_all.at[me], target).start()
 
     db = db_send[row].astype(f32)
-    for step in range(1, n):
-        other = lax.rem(row + step, n)
+    for other in near[1:]:
         db_copy(other, other).wait_recv()
         db = db + db_recv[other].astype(f32)
     db = db.reshape(size, width)
-    pb_v = proj_ref[:, 3 * width : 4 * width]
-    d_bg = (db * pb_v * mask * sig_b * (1.0 - sig_b)).astype(bf16)
-    d_bv = (db * sig_b * mask).astype(bf16)
-    scatter_weights(
-        2,
-        jnp.dot(zn_t, d_bg, preferred_element_type=f32),
-        jnp.dot(zn_t, d_bv, preferred_element_type=f32),
-    )
-    gather_weights(1)
+    d_bg = (db * slope_g[row]).astype(bf16)
+    d_bv = (db * slope_v[row]).astype(bf16)
     dzn = dzn + dot_t(d_bg, w_in_ref[:, 2 * width : 3 * width])
     dzn = dzn + dot_t(d_bv, w_in_ref[:, 3 * width : 4 * width])
-    scaled = dzn * gain_in
+    zhat, zinv = normed(row)
+    scaled = dzn * gain_in_ref[...]
     pair_grad = zinv * (scaled - last_mean(scaled) - zhat * last_mean(scaled * zhat))
     pair_grad_ref[...] = pair_grad.astype(bf16).reshape(blk, blk, width)
-    gather_weights(2)
-    grad_gate_ref[...], grad_out_ref[...] = finish_weights(0)
-    grad_in_ref[:, 0:width], grad_in_ref[:, width : 2 * width] = finish_weights(1)
-    grad_in_ref[:, 2 * width : 3 * width], grad_in_ref[:, 3 * width : 4 * width] = finish_weights(2)
 
     for step in range(1, n):
-        b_copy(row, lax.rem(row + step, n)).wait_send()
+        pair_copy(row, lax.rem(row + step, n)).wait_send()
         dx_copy(col, lax.rem(col + step, n)).wait_send()
         x_copy(lax.rem(col + step, n), col).wait_send()
         db_copy(lax.rem(row + step, n), row).wait_send()
-
-    @pl.loop(1, total)
-    def _(step):
-        other, target = peer(step)
-        for group in range(3):
-            ws_copy(group, other, target, me).wait_send()
-            wg_copy(group, other, target, me).wait_send()
+    w_stage(0, w0_part).wait_send()
+    w_stage(1, w1_part).wait_send()
+    w_stage(2, w_all).wait_recv()
+    early = w_all[:, 0:share].reshape(2 * width, width).astype(f32)
+    grad_gate_ref[...], grad_out_ref[...] = early[:width], early[width:]
+    late = w_all[:, share : 3 * share].reshape(4 * width, width).astype(f32)
+    for at in range(4):
+        grad_in_ref[:, at * width : (at + 1) * width] = late[at * width : (at + 1) * width]
+    w_stage(2, w_all).wait_send()
+
+
+def store_kernel(*refs):
+    sources, targets, sems = refs[:5], refs[5:10], refs[10]
+    copies = [
+        pltpu.make_async_copy(source, target, sems.at[at])
+        for at, (source, target) in enumerate(zip(sources, targets))
+    ]
+    for copy in copies:
+        copy.start()
+    for copy in copies:
+        copy.wait()
 
 
 def fused_plan(n, pair, cotangent, crop_length, gain_in, w_in, w_gate, product_norm_gain, w_out):
@@ -383,19 +427,22 @@
     f32, bf16 = jnp.float32, jnp.bfloat16
     shape = jax.ShapeDtypeStruct
     blocks = (n, blk, blk, width)
-    shares = (3, total, share, width)
+    grad = lambda rows: pltpu.VMEM((total, rows, width), bf16)
+    slope = pltpu.VMEM((n, blk * blk, width), f32)
     dma = pltpu.SemaphoreType.DMA
     vmem = pl.BlockSpec(memory_space=pltpu.VMEM)
-    return pl.pallas_call(
+    hbm = pl.BlockSpec(memory_space=pltpu.HBM)
+    out_shape = (
+        shape(pair.shape, bf16),
+        shape(pair.shape, bf16),
+        shape(w_in.shape, f32),
+        shape(w_gate.shape, f32),
+        shape(w_out.shape, f32),
+    )
+    results = pl.pallas_call(
         functools.partial(fused_kernel, n),
-        out_shape=(
-            shape(pair.shape, bf16),
-            shape(pair.shape, bf16),
-            shape(w_in.shape, f32),
-            shape(w_gate.shape, f32),
-            shape(w_out.shape, f32),
-        ),
-        in_specs=[pl.BlockSpec(memory_space=pltpu.SMEM)] + [vmem] * 7,
+        out_shape=out_shape,
+        in_specs=[pl.BlockSpec(memory_space=pltpu.SMEM)] + [hbm] * 7,
         out_specs=(vmem,) * 5,
         scratch_shapes=[
             pltpu.VMEM(blocks, bf16),
@@ -404,20 +451,33 @@
             pltpu.VMEM(blocks, bf16),
             pltpu.VMEM(blocks, bf16),
             pltpu.VMEM(blocks, bf16),
-            pltpu.VMEM(shares, bf16),
-            pltpu.VMEM(shares, bf16),
-            pltpu.VMEM(shares, bf16),
+            pltpu.VMEM(blocks, bf16),
+            grad(share),
+            grad(share),
+            grad(2 * share),
+            grad(2 * share),
+            grad(3 * share),
+            pltpu.VMEM((n, width, blk * blk), bf16),
+            slope,
+            slope,
+            pltpu.VMEM((2, width, width), f32),
+            pltpu.VMEM(pair.shape, bf16),
+            pltpu.VMEM((1, width), f32),
+            pltpu.VMEM(w_in.shape, bf16),
+            pltpu.VMEM(w_gate.shape, bf16),
+            pltpu.VMEM((1, width), f32),
+            pltpu.VMEM(w_out.shape, bf16),
             pltpu.VMEM(blocks[1:], f32),
             pltpu.VMEM(blocks[1:], f32),
             pltpu.VMEM(blocks[1:], f32),
             pltpu.VMEM(blocks[1:], f32),
-            pltpu.VMEM((blk * blk, 4 * width), f32),
-            pltpu.VMEM((width, blk * blk), bf16),
+            pltpu.VMEM((blk * blk, 2 * width), f32),
         ]
         + [dma((n,))] * 8
-        + [dma((3, total))] * 4,
+        + [dma((3,))] * 2
+        + [dma((7,))],
         compiler_params=pltpu.CompilerParams(
-            collective_id=0, has_side_effects=True, vmem_limit_bytes=40 * 1024 * 1024
+            collective_id=0, has_side_effects=True, vmem_limit_bytes=VMEM_GRANT
         ),
     )(
         crop_length,
@@ -429,6 +489,13 @@
         product_norm_gain.reshape(1, width),
         w_out,
     )
+    return pl.pallas_call(
+        store_kernel,
+        out_shape=out_shape,
+        in_specs=[vmem] * 5,
+        out_specs=(hbm,) * 5,
+        scratch_shapes=[dma((5,))],
+    )(*results)
 
 
 def choose_plan(n_rows, n_cols, pair, cotangent, crop_length, gain_in, w_in, w_gate, product_norm_gain, w_out):

time: 54 us -> 46.3 us (0.86)
  local copies, waits for them, and re-layouts: 7.97 us -> 0 us
    unnamed x19 -> x0, local copies, waits for them, and re-layouts: 7.97 us -> none
    pallas_call x1 -> x2, Pallas kernels: 44.4 us -> 44.8 us  [the longest x1 42.9 us: fused_plan(): pl.pallas_call(functools.partial(fused_kernel, n), out_shape=out_shape, i...]
where the time goes in v2:
time: 46.3 us; the launch traced here: 46.1 us
  Pallas kernels  44.8 us (97%)
  between operations  1.29 us (3%)
    pallas_call x1, Pallas kernels, fused_plan(): pl.pallas_call(functools.partial(fused_kernel, n), out_shape=out_shape, i...  42.9 us
    pallas_call x1, Pallas kernels, fused_plan(): pl.pallas_call(store_kernel, out_shape=out_shape, in_specs=[vmem] * 5, ou...  1.89 us

profile of v2, /device:TPU:0, one launch (start us, length us, event | category | flops | bytes accessed | tf_op | source)
XLA Modules:
  0.0 46.1 jit_solution(4572513750547429676)
XLA Ops:
  1.3 42.9 %shard_map.119 = (bf16[16,16,128]{2,1,0:T(8,128)(2,1)}, bf16[16,16,128]{2,1,0:T(8,128)(2,1)}, f32[128,512]{1,0:T(8,128)}, f32[128,128]{1,0:T(8,128)}, f32[128,128]{1,0:T(8,128)}) custom-call(s32[1]{0:T(128)S(6)} %copy.13.crop_ref, bf16[16,16,128]{2,1,0:T(8,128)(2,1)} %pair_hbm.1, bf16[16,16,128]{2,1,0:T(8,128)(2,1)} %cot_hbm.1, f32[1,128]{1,0:T(1,128)} %bitcast.2, ...), custom_call_target="tpu_custom_call" | custom-call | tf_op jit(solution)/shard_map/pallas_call | solution.py:442
  44.2 1.9 %shard_map.120 = (bf16[16,16,128]{2,1,0:T(8,128)(2,1)}, bf16[16,16,128]{2,1,0:T(8,128)(2,1)}, f32[128,512]{1,0:T(8,128)}, f32[128,128]{1,0:T(8,128)}, f32[128,128]{1,0:T(8,128)}) custom-call(bf16[16,16,128]{2,1,0:T(8,128)(2,1)} %get-tuple-element.10.refs_0_, bf16[16,16,128]{2,1,0:T(8,128)(2,1)} %get-tuple-element.11.refs_1_, ...), custom_call_target="tpu_custom_call" | custom-call | tf_op jit(solution)/shard_map/pallas_call | solution.py:492

commit v3 on v2

--- a/solution.py
+++ b/solution.py
@@ -126,10 +126,8 @@
     dx_all,
     db_send,
     db_recv,
-    w0_part,
-    w0_recv,
-    w1_part,
-    w1_recv,
+    w_part,
+    w_recv,
     w_all,
     zn_all,
     slope_g,
@@ -167,9 +165,12 @@
     col = lax.axis_index("cols")
     me = row * n + col
 
-    def peer(step):
-        other = lax.rem(me + step, total)
-        return other, {"rows": lax.div(other, n), "cols": lax.rem(other, n)}
+    def peer(steps):
+        to_row, to_col = lax.rem(row + steps[0], n), lax.rem(col + steps[1], n)
+        return to_row * n + to_col, {"rows": to_row, "cols": to_col}
+
+    far_first = sorted(range(1, n), key=lambda step: -min(step, n - step))
+    peers = [(r, c) for c in far_first + [0] for r in range(n) if r + c > 0]
 
     def nearest(place):
         for step in range(0, n, 2):
@@ -195,7 +196,7 @@
         fetch.start()
 
     barrier = pltpu.get_barrier_semaphore()
-    for step in range(1, total):
+    for step in peers:
         _, target = peer(step)
         pl.semaphore_signal(barrier, inc=1, device_id=target, device_id_type=MESH)
 
@@ -226,10 +227,10 @@
 
     def w_stage(stage, buffer):
         piece = buffer.at[pl.ds(0, total - 1)]
-        return w_copy(stage, piece, piece, peer(1)[1])
+        return w_copy(stage, piece, piece, peer(peers[0])[1])
 
     def scatter_weights(stage, outgoing, arriving):
-        for step in range(1, total):
+        for step in peers:
             other, target = peer(step)
             w_copy(stage, outgoing.at[other], arriving.at[me], target).start()
         arriving[me] = outgoing[me]
@@ -282,7 +283,7 @@
             prepare(block)
         right_f[...] = jnp.swapaxes(b_all[block].astype(f32), 0, 1)
 
-        @pl.loop(0, blk)
+        @pl.loop(0, blk, unroll=4)
         def _(i):
             line = left_f[i]
             x_send[block, i] = jnp.sum(line[:, None, :] * right_f[...], axis=0).astype(bf16)
@@ -311,23 +312,22 @@
     scaled = dot_t(dq, w_out) * gain_x
     dx = xinv * (scaled - last_mean(scaled) - xhat * last_mean(scaled * xhat))
     dx_all[col] = dx.astype(bf16).reshape(blk, blk, width)
-    for step in range(1, n):
+    for step in far_first:
         dx_copy(col, lax.rem(col + step, n)).start()
     q_out = jnp.dot(xn_f.astype(bf16), w_out, preferred_element_type=f32)
     update_ref[...] = (sig_g * q_out).astype(bf16).reshape(blk, blk, width)
     dg = (cot * q_out * sig_g * (1.0 - sig_g)).astype(bf16)
     zn_t = zn_all[row]
     half = total // 2
-    w0_part[0:half] = (
+    w_part[0:half, 0:share] = (
         jnp.dot(zn_t, dg, preferred_element_type=f32).astype(bf16).reshape(half, share, width))
-    w0_part[half:total] = (
+    w_part[half:total, 0:share] = (
         jnp.dot(xn_f.T.astype(bf16), dq, preferred_element_type=f32)
         .astype(bf16).reshape(half, share, width))
-    scatter_weights(0, w0_part, w0_recv)
 
     da_f[...] = jnp.zeros_like(da_f)
     b_sums[...] = jnp.zeros_like(b_sums)
-    for step in range(n):
+    for step in [0] + far_first[::-1]:
         block = lax.rem(col + step, n)
         if step > 0:
             dx_copy(block, block).wait_recv()
@@ -339,7 +339,7 @@
             da_f[i] += jnp.sum(line * right_f[...], axis=0)
             return db + line * left_f[i][None]
 
-        db = lax.fori_loop(0, blk, over_i, jnp.zeros((blk, blk, width), f32))
+        db = lax.fori_loop(0, blk, over_i, jnp.zeros((blk, blk, width), f32), unroll=2)
         db_send[block] = db.astype(bf16)
 
         @pl.when(block != row)
@@ -365,18 +365,16 @@
         b_sums[1],
     )
     for at, term in enumerate(sums):
-        w1_part[at * quarter : (at + 1) * quarter] = (
+        w_part[at * quarter : (at + 1) * quarter, share : 3 * share] = (
             term.astype(bf16).reshape(quarter, 2 * share, width))
-    scatter_weights(1, w1_part, w1_recv)
+    scatter_weights(0, w_part, w_recv)
     dzn = dot_t(dg, w_gate_ref[...]) + dot_t(d_ag, w_in_ref[:, 0:width])
     dzn = dzn + dot_t(d_av, w_in_ref[:, width : 2 * width])
-    w_stage(0, w0_recv).wait_recv()
-    w_all[me, 0:share] = jnp.sum(w0_recv[...].astype(f32), axis=0).astype(bf16)
-    w_stage(1, w1_recv).wait_recv()
-    w_all[me, share : 3 * share] = jnp.sum(w1_recv[...].astype(f32), axis=0).astype(bf16)
-    for step in range(1, total):
+    w_stage(0, w_recv).wait_recv()
+    w_all[me] = jnp.sum(w_recv[...].astype(f32), axis=0).astype(bf16)
+    for step in peers:
         _, target = peer(step)
-        w_copy(2, w_all.at[me], w_all.at[me], target).start()
+        w_copy(1, w_all.at[me], w_all.at[me], target).start()
 
     db = db_send[row].astype(f32)
     for other in near[1:]:
@@ -397,15 +395,14 @@
         dx_copy(col, lax.rem(col + step, n)).wait_send()
         x_copy(lax.rem(col + step, n), col).wait_send()
         db_copy(lax.rem(row + step, n), row).wait_send()
-    w_stage(0, w0_part).wait_send()
-    w_stage(1, w1_part).wait_send()
-    w_stage(2, w_all).wait_recv()
+    w_stage(0, w_part).wait_send()
+    w_stage(1, w_all).wait_recv()
     early = w_all[:, 0:share].reshape(2 * width, width).astype(f32)
     grad_gate_ref[...], grad_out_ref[...] = early[:width], early[width:]
     late = w_all[:, share : 3 * share].reshape(4 * width, width).astype(f32)
     for at in range(4):
         grad_in_ref[:, at * width : (at + 1) * width] = late[at * width : (at + 1) * width]
-    w_stage(2, w_all).wait_send()
+    w_stage(1, w_all).wait_send()
 
 
 def store_kernel(*refs):
@@ -452,10 +449,8 @@
             pltpu.VMEM(blocks, bf16),
             pltpu.VMEM(blocks, bf16),
             pltpu.VMEM(blocks, bf16),
-            grad(share),
-            grad(share),
-            grad(2 * share),
-            grad(2 * share),
+            grad(3 * share),
+            grad(3 * share),
             grad(3 * share),
             pltpu.VMEM((n, width, blk * blk), bf16),
             slope,
@@ -474,7 +469,7 @@
             pltpu.VMEM((blk * blk, 2 * width), f32),
         ]
         + [dma((n,))] * 8
-        + [dma((3,))] * 2
+        + [dma((2,))] * 2
         + [dma((7,))],
         compiler_params=pltpu.CompilerParams(
             collective_id=0, has_side_effects=True, vmem_limit_bytes=VMEM_GRANT

time: 46.3 us -> 43.1 us (0.931)
  Pallas kernels: 44.8 us -> 41.6 us
    pallas_call x1, Pallas kernels: 42.9 us -> 39.7 us  [fused_plan(): pl.pallas_call(functools.partial(fused_kernel, n), out_shape=out_shape, i...]
where the time goes in v3:
time: 43.1 us; the launch traced here: 42.9 us
  Pallas kernels  41.6 us (97%)
  between operations  1.29 us (3%)
    pallas_call x1, Pallas kernels, fused_plan(): pl.pallas_call(functools.partial(fused_kernel, n), out_shape=out_shape, i...  39.7 us
    pallas_call x1, Pallas kernels, fused_plan(): pl.pallas_call(store_kernel, out_shape=out_shape, in_specs=[vmem] * 5, ou...  1.89 us

profile of v3, /device:TPU:0, one launch (start us, length us, event | category | flops | bytes accessed | tf_op | source)
XLA Modules:
  0.0 42.9 jit_solution(10766856296009213128)
XLA Ops:
  1.3 39.7 %shard_map.119 = (bf16[16,16,128]{2,1,0:T(8,128)(2,1)}, bf16[16,16,128]{2,1,0:T(8,128)(2,1)}, f32[128,512]{1,0:T(8,128)}, f32[128,128]{1,0:T(8,128)}, f32[128,128]{1,0:T(8,128)}) custom-call(s32[1]{0:T(128)S(6)} %copy.13.crop_ref, bf16[16,16,128]{2,1,0:T(8,128)(2,1)} %pair_hbm.1, bf16[16,16,128]{2,1,0:T(8,128)(2,1)} %cot_hbm.1, f32[1,128]{1,0:T(1,128)} %bitcast.2, ...), custom_call_target="tpu_custom_call" | custom-call | tf_op jit(solution)/shard_map/pallas_call | solution.py:439
  41.0 1.9 %shard_map.120 = (bf16[16,16,128]{2,1,0:T(8,128)(2,1)}, bf16[16,16,128]{2,1,0:T(8,128)(2,1)}, f32[128,512]{1,0:T(8,128)}, f32[128,128]{1,0:T(8,128)}, f32[128,128]{1,0:T(8,128)}) custom-call(bf16[16,16,128]{2,1,0:T(8,128)(2,1)} %get-tuple-element.10.refs_0_, bf16[16,16,128]{2,1,0:T(8,128)(2,1)} %get-tuple-element.11.refs_1_, ...), custom_call_target="tpu_custom_call" | custom-call | tf_op jit(solution)/shard_map/pallas_call | solution.py:487

commit v4 on v3

--- a/solution.py
+++ b/solution.py
@@ -258,10 +258,16 @@
         gated = jax.nn.sigmoid(pb[:, :width]) * mask
         right = (gated * pb[:, width:]).astype(bf16)
         b_all[block] = right.reshape(blk, blk, width)
-        zn_all[block] = zn_f.T.astype(bf16)
+        slope_g[block] = pb[:, :width]
+        slope_v[block] = pb[:, width:]
+        return zn
+
+    def prepare_backward(block):
+        zn_all[block] = (normed(block)[0] * gain_in_ref[...]).T.astype(bf16)
+        sig = jax.nn.sigmoid(slope_g[block])
+        gated = sig * mask_of(block)
+        slope_g[block] = gated * slope_v[block] * (1.0 - sig)
         slope_v[block] = gated
-        slope_g[block] = gated * pb[:, width:] * (1.0 - jax.nn.sigmoid(pb[:, :width]))
-        return zn
 
     for fetch in fetches[:4]:
         fetch.wait()
@@ -292,6 +298,8 @@
         def _():
             x_copy(block, col).start()
 
+    for block in near:
+        prepare_backward(block)
     x = x_send[col].astype(f32)
     for step in range(1, n):
         other = lax.rem(col + step, n)

time: 43.1 us -> 43.1 us (level)
  no operation moved by 1% of the time
where the time goes in v4:
time: 43.1 us; the launch traced here: 42.9 us
  Pallas kernels  41.6 us (97%)
  between operations  1.29 us (3%)
    pallas_call x1, Pallas kernels, fused_plan(): pl.pallas_call(functools.partial(fused_kernel, n), out_shape=out_shape, i...  39.7 us
    pallas_call x1, Pallas kernels, fused_plan(): pl.pallas_call(store_kernel, out_shape=out_shape, in_specs=[vmem] * 5, ou...  1.89 us

profile of v4, /device:TPU:0, one launch (start us, length us, event | category | flops | bytes accessed | tf_op | source)
XLA Modules:
  0.0 42.9 jit_solution(11546844749356499714)
XLA Ops:
  1.3 39.7 %shard_map.119 = (bf16[16,16,128]{2,1,0:T(8,128)(2,1)}, bf16[16,16,128]{2,1,0:T(8,128)(2,1)}, f32[128,512]{1,0:T(8,128)}, f32[128,128]{1,0:T(8,128)}, f32[128,128]{1,0:T(8,128)}) custom-call(s32[1]{0:T(128)S(6)} %copy.13.crop_ref, bf16[16,16,128]{2,1,0:T(8,128)(2,1)} %pair_hbm.1, bf16[16,16,128]{2,1,0:T(8,128)(2,1)} %cot_hbm.1, f32[1,128]{1,0:T(1,128)} %bitcast.2, ...), custom_call_target="tpu_custom_call" | custom-call | tf_op jit(solution)/shard_map/pallas_call | solution.py:447
  41.0 1.9 %shard_map.120 = (bf16[16,16,128]{2,1,0:T(8,128)(2,1)}, bf16[16,16,128]{2,1,0:T(8,128)(2,1)}, f32[128,512]{1,0:T(8,128)}, f32[128,128]{1,0:T(8,128)}, f32[128,128]{1,0:T(8,128)}) custom-call(bf16[16,16,128]{2,1,0:T(8,128)(2,1)} %get-tuple-element.10.refs_0_, bf16[16,16,128]{2,1,0:T(8,128)(2,1)} %get-tuple-element.11.refs_1_, ...), custom_call_target="tpu_custom_call" | custom-call | tf_op jit(solution)/shard_map/pallas_call | solution.py:495
